TPU v7x, 512 devices: a whole 4x8x8 slice. The times are simulated.
512 devices in a mesh: expert: 8 (over x, y_hi), dp: 64 (over z, y_lo, core).
Axes of the slice: x: 4, y: 8 (y_hi: 2, y_lo: 4; y = y_hi * 4 + y_lo), z: 8, core: 2. Of those that a mesh axis runs over, the one named last changes fastest.
Arguments:
- tokens: bfloat16 [64, 16, 2048], P('dp', 'expert'), may hold values from -6 to 6
- out_grad: bfloat16 [64, 16, 2048], P('dp', 'expert'), may hold values from -6 to 6
- expert_ids: int32 [64, 16, 2], P('dp'), may hold values from 0 to 7, as said below
- gate_scores: bfloat16 [64, 16, 2], P('dp'), may hold values from 0.25 to 1
- w_gate: bfloat16 [8, 2048, 8192], P('expert', None, 'dp'), may hold values from -0.125 to 0.125
- w_up: bfloat16 [8, 2048, 8192], P('expert', None, 'dp'), may hold values from -0.125 to 0.125
- w_down: bfloat16 [8, 8192, 2048], P('expert', 'dp'), may hold values from -0.0625 to 0.0625
Outputs:
- token_grad: bfloat16 [64, 16, 2048], P('dp', 'expert')
- grad_gate: bfloat16 [8, 2048, 8192], P('expert', None, 'dp')
- grad_up: bfloat16 [8, 2048, 8192], P('expert', None, 'dp')
- grad_down: bfloat16 [8, 8192, 2048], P('expert', 'dp')
Inputs may be any that keep to these rules, and one draw needn't show every extreme that they name: `expert_ids`: each token names two different experts; within a group no expert is named by more than 7 tokens, and in every group some expert is named by exactly 7 tokens.
All inputs are finite; a program needn't handle non-finite values.
Results may differ from a plain program's by a relative error of at most 0.0058.
Values may be sent and summed in bfloat16 or wider, within the bound.
A program may use at most 64 MiB of HBM per device.

v0:
```python
import jax
import jax.numpy as jnp
from jax import lax
from jax.sharding import PartitionSpec as P


def slot_table(expert_ids, experts):
    expert_range = jnp.arange(experts, dtype=jnp.int32)
    naming = jnp.sum((expert_ids[..., :, None] == expert_range).astype(jnp.int32), axis=-2)
    before = jnp.cumsum(naming, axis=-2) - naming
    return jnp.take_along_axis(before, expert_ids, axis=-1)


def local(tokens, out_grad, expert_ids, gate_scores, w_gate, w_up, w_down):
    tok_dev = tokens.shape[1]
    group_tok = expert_ids.shape[1]
    capacity = min(2 * tok_dev + 3, group_tok)
    experts = lax.axis_size("expert")
    my_expert = lax.axis_index("expert")
    group_ids = expert_ids[0]
    group_slots = slot_table(group_ids, experts)
    group_x, group_dy = (
        lax.all_gather(tokens, "expert", axis=1, tiled=True),
        lax.all_gather(out_grad, "expert", axis=1, tiled=True),
    )
    slot_range = jnp.arange(capacity, dtype=jnp.int32)
    matches = (group_ids[None, :, :] == my_expert) & (
        group_slots[None, :, :] == slot_range[:, None, None]
    )
    placing = jnp.sum(matches.astype(jnp.float32), axis=-1)
    weighting = jnp.sum(
        matches.astype(jnp.float32) * gate_scores[0].astype(jnp.float32)[None, :, :], axis=-1
    )
    x_picked = jnp.dot(
        placing.astype(jnp.bfloat16), group_x[0], preferred_element_type=jnp.float32
    ).astype(jnp.bfloat16)
    dy_picked = jnp.dot(
        weighting.astype(jnp.bfloat16), group_dy[0], preferred_element_type=jnp.float32
    ).astype(jnp.bfloat16)
    gate_slab = w_gate[0]
    up_slab = w_up[0]
    down_slab = w_down[0]
    input_rows = lax.all_gather(x_picked, "dp", axis=0, tiled=True)
    pre_gate = jnp.dot(input_rows, gate_slab, preferred_element_type=jnp.float32)
    pre_up = jnp.dot(input_rows, up_slab, preferred_element_type=jnp.float32)
    sigmoid_gate = jax.nn.sigmoid(pre_gate)
    activated = pre_gate * sigmoid_gate
    hidden = (activated * pre_up).astype(jnp.bfloat16)
    grad_rows = lax.all_gather(dy_picked, "dp", axis=0, tiled=True)
    grad_down = jnp.dot(hidden.T, grad_rows, preferred_element_type=jnp.float32).astype(
        jnp.bfloat16
    )
    grad_hidden = jnp.dot(grad_rows, down_slab.T, preferred_element_type=jnp.float32)
    gate_delta = (
        grad_hidden * pre_up * sigmoid_gate * (1.0 + pre_gate * (1.0 - sigmoid_gate))
    ).astype(jnp.bfloat16)
    up_delta = (grad_hidden * activated).astype(jnp.bfloat16)
    grad_gate = jnp.dot(input_rows.T, gate_delta, preferred_element_type=jnp.float32).astype(
        jnp.bfloat16
    )
    grad_up = jnp.dot(input_rows.T, up_delta, preferred_element_type=jnp.float32).astype(
        jnp.bfloat16
    )
    total = jnp.dot(gate_delta, gate_slab.T, preferred_element_type=jnp.float32)
    row_grad = lax.psum_scatter(
        total + jnp.dot(up_delta, up_slab.T, preferred_element_type=jnp.float32),
        "dp",
        scatter_dimension=0,
        tiled=True,
    )
    partial_tokens = jnp.dot(
        placing.T, row_grad, precision=lax.Precision.HIGHEST, preferred_element_type=jnp.float32
    )
    token_grad = lax.psum_scatter(partial_tokens, "expert", scatter_dimension=0, tiled=True)
    return (token_grad.astype(jnp.bfloat16)[None], grad_gate[None], grad_up[None], grad_down[None])


def solution(mesh):
    return jax.shard_map(
        local,
        mesh=mesh,
        in_specs=(
            P("dp", "expert", None),
            P("dp", "expert", None),
            P("dp", None, None),
            P("dp", None, None),
            P("expert", None, "dp"),
            P("expert", None, "dp"),
            P("expert", "dp", None),
        ),
        out_specs=(
            P("dp", "expert", None),
            P("expert", None, "dp"),
            P("expert", None, "dp"),
            P("expert", "dp", None),
        ),
        check_vma=False,
    )
```

profile of v0, /device:TPU:64, one launch (start us, length us, event | category | flops | bytes accessed | tf_op | source)
XLA Modules:
  0.0 564.1 jit_solution(10592391072857889739)
XLA Ops:
  7.2 0.0 copy-start
  7.2 0.0 all-gather.7.cloned.1.call-start
  7.2 0.7 fusion.30
  8.0 0.7 compare_bitcast_fusion
  8.6 0.7 bitcast_convert_fusion
  9.3 0.7 convert_reduce_fusion
  10.0 0.1 copy.70
  10.1 0.1 copy.72
  10.2 0.1 reshape.47
  10.3 0.0 copy-start.6
  10.3 0.0 copy-start.7
  10.3 0.7 gather_fusion
  11.0 0.1 gather.7
  11.1 0.1 copy.73
  11.2 0.0 copy-done.5
  11.2 0.0 copy-done.6
  11.2 44.1 %all_gather.14 = bf16[1,16,2048]{2,0,1:T(2,128)(2,1)S(1)} all-gather(bf16[1,2,2048]{2,0,1:T(2,128)(2,1)S(1)} %copy.75), channel_id=1, replica_groups=mesh['expert'=8,'dp'=64] {'expert'}, dimensions={1}, use_global_device_ids=true | all-gather | bytes 73728 | tf_op jit(solution)/shard_map/all_gather | solution.py:23
  55.4 0.8 fusion.5
  56.2 0.0 all-gather.7.cloned.1.call-update
  56.2 0.0 all-gather.5.cloned.1.call-start
  56.3 0.0 copy-done.7
  56.3 44.0 %all_gather.12 = bf16[1,16,2048]{2,0,1:T(2,128)(2,1)S(1)} all-gather(bf16[1,2,2048]{2,0,1:T(2,128)(2,1)S(1)} %copy.74), channel_id=1, replica_groups=mesh['expert'=8,'dp'=64] {'expert'}, dimensions={1}, use_global_device_ids=true | all-gather | bytes 73728 | tf_op jit(solution)/shard_map/all_gather | solution.py:24
  100.3 0.8 fusion.4
  101.1 0.0 all-gather.5.cloned.1.call-update
  101.1 1.3 dynamic-slice.6
  102.4 1.3 dynamic-slice.2
  104.9 71.9 %all-gather.7.cloned.1.call-done = bf16[64,7,2048]{2,1,0:T(8,128)(2,1)} async-done(((bf16[1,7,2048]{2,1,0:T(8,128)(2,1)}), bf16[64,7,2048]{2,1,0:T(8,128)(2,1)}) %all-gather.7.cloned.1.call-update) | async-done | bytes 1835024 | tf_op jit(solution)/shard_map/all_gather | solution.py:43
  176.8 2.6 reshape.57
  179.4 0.0 copy-start.2
  179.4 0.6 fusion.8
  180.1 0.4 copy-done.2
  180.5 0.6 fusion.11
  181.1 114.7 %all-gather.5.cloned.1.call-done = bf16[64,7,2048]{2,1,0:T(8,128)(2,1)} async-done(((bf16[1,7,2048]{2,1,0:T(8,128)(2,1)}), bf16[64,7,2048]{2,1,0:T(8,128)(2,1)}) %all-gather.5.cloned.1.call-update) | async-done | bytes 1835024 | tf_op jit(solution)/shard_map/all_gather | solution.py:49
  295.8 3.7 reshape.55
  299.6 2.9 fusion.3
  302.5 0.0 copy-done.1
  302.5 0.6 multiply_convert_fusion.1
  303.2 0.0 copy-start.3
  303.2 0.6 fusion.6
  303.8 2.4 convolution_add_fusion
  306.3 143.5 %fusion = f32[8,2048]{1,0:T(8,128)S(1)} fusion(f32[448,2048]{1,0:T(8,128)} %convolution_add_fusion), kind=kCustom, calls=%all-reduce-scatter | all-reduce-scatter fusion | flops 1048577 | bytes 3737600
  449.8 0.0 copy-start.4
  449.8 2.1 collective-permute-start.6
  451.9 1.9 collective-permute-start.5
  453.8 17.8 %collective-permute-start.7 = (f32[7,2048]{1,0:T(8,128)S(1)}, f32[7,2048]{1,0:T(8,128)S(1)}, u32[]{:S(2)}, u32[]{:S(2)}) collective-permute-start(f32[7,2048]{1,0:T(8,128)S(1)} %slice.2), channel_id=1, source_target_pairs={{0,8},{1,9},{2,10},{3,11},{4,12},{5,13},{6,14},{7,15},{8,16},{9,17... | collective-permute-start | bytes 172040
  471.7 1.6 fusion.2
  473.3 5.9 %collective-permute-start.4 = (f32[8,2048]{1,0:T(8,128)S(1)}, f32[8,2048]{1,0:T(8,128)S(1)}, u32[]{:S(2)}, u32[]{:S(2)}) collective-permute-start(f32[8,2048]{1,0:T(8,128)S(1)} %fusion), channel_id=1, source_target_pairs={{0,5},{1,6},{2,7},{3,8},{4,9},{5,10},{6,11},{7,12},{8,13},{9,14},{... | collective-permute-start | bytes 196616
  479.2 8.7 %collective-permute-start.3 = (f32[8,2048]{1,0:T(8,128)S(1)}, f32[8,2048]{1,0:T(8,128)S(1)}, u32[]{:S(2)}, u32[]{:S(2)}) collective-permute-start(f32[8,2048]{1,0:T(8,128)S(1)} %fusion), channel_id=1, source_target_pairs={{0,4},{1,5},{2,6},{3,7},{4,8},{5,9},{6,10},{7,11},{8,12},{9,13},{1... | collective-permute-start | bytes 196616
  487.8 0.0 collective-permute-done.7
  487.8 1.9 collective-permute-start.2
  489.8 0.0 collective-permute-done.6
  489.8 3.4 collective-permute-start.1
  493.2 0.0 collective-permute-done.5
  493.2 2.3 collective-permute-start
  495.5 1.6 fusion.1
  497.1 0.0 collective-permute-done.4
  497.1 0.0 collective-permute-done.3
  497.1 0.0 collective-permute-done.2
  497.1 1.7 collective-permute-done.1
  498.8 2.7 collective-permute-done
  501.4 1.0 concatenate.3
  502.5 0.4 fusion.16
  502.9 53.8 %all-reduce.4 = bf16[16,2048]{1,0:T(8,128)(2,1)S(1)} all-reduce(f32[16,2048]{1,0:T(8,128)S(1)} %fusion.16), channel_id=3, replica_groups=mesh['expert'=8,'dp'=64] {'expert'}, use_global_device_ids=true, to_apply=%region_5.6.clone | all-reduce | flops 32768 | bytes 196608
  556.6 0.6 fusion.23
  (14 shorter events, 0.1 us)
Async XLA Ops:
  7.2 172.3 %copy-start = (bf16[1,2048,128]{2,1,0:T(8,128)(2,1)S(1)}, bf16[1,2048,128]{2,1,0:T(8,128)(2,1)}, u32[]{:S(2)}) copy-start(bf16[1,2048,128]{2,1,0:T(8,128)(2,1)} %param.11) | copy-start | bytes 1572868
  7.2 169.6 %all-gather.7.cloned.1.call-start = ((), (), s32[]{:S(2)}) async-start(), calls=%async_computation.1 | async-start | bytes 2129920 | tf_op jit(solution)/shard_map/all_gather | solution.py:43
  10.3 0.9 copy-start.5
  10.3 0.9 copy-start.6
  10.3 46.0 %copy-start.7 = (bf16[1,2,2048]{2,1,0:T(2,128)(2,1)S(1)}, bf16[1,2,2048]{2,1,0:T(2,128)(2,1)}, u32[]{:S(2)}) copy-start(bf16[1,2,2048]{2,1,0:T(2,128)(2,1)} %param.8) | copy-start | bytes 24580
  56.2 239.6 %all-gather.5.cloned.1.call-start = ((), (), s32[]{:S(2)}) async-start(), calls=%async_computation | async-start | bytes 2129920 | tf_op jit(solution)/shard_map/all_gather | solution.py:49
  179.4 1.0 copy-start.2
  299.6 3.0 copy-start.1
  299.6 3.0 copy-start.8
  303.2 0.7 copy-start.3
  449.8 45.7 %copy-start.4 = (bf16[448,128]{1,0:T(8,128)(2,1)S(1)}, bf16[448,128]{1,0:T(8,128)(2,1)}, u32[]{:S(2)}) copy-start(bf16[448,128]{1,0:T(8,128)(2,1)} %copy-done.3) | copy-start | bytes 344068
  449.8 39.9 %collective-permute-start.6 = (f32[8,2048]{1,0:T(8,128)S(1)}, f32[8,2048]{1,0:T(8,128)S(1)}, u32[]{:S(2)}, u32[]{:S(2)}) collective-permute-start(f32[8,2048]{1,0:T(8,128)S(1)} %fusion), channel_id=1, source_target_pairs={{0,7},{1,8},{2,9},{3,10},{4,11},{5,12},{6,13},{7,14},{8,15},{9,16}... | collective-permute-start | bytes 196616
  451.9 41.2 %collective-permute-start.5 = (f32[8,2048]{1,0:T(8,128)S(1)}, f32[8,2048]{1,0:T(8,128)S(1)}, u32[]{:S(2)}, u32[]{:S(2)}) collective-permute-start(f32[8,2048]{1,0:T(8,128)S(1)} %fusion), channel_id=1, source_target_pairs={{0,6},{1,7},{2,8},{3,9},{4,10},{5,11},{6,12},{7,13},{8,14},{9,15},... | collective-permute-start | bytes 196616
  453.8 34.0 %collective-permute-start.7 = (f32[7,2048]{1,0:T(8,128)S(1)}, f32[7,2048]{1,0:T(8,128)S(1)}, u32[]{:S(2)}, u32[]{:S(2)}) collective-permute-start(f32[7,2048]{1,0:T(8,128)S(1)} %slice.2), channel_id=1, source_target_pairs={{0,8},{1,9},{2,10},{3,11},{4,12},{5,13},{6,14},{7,15},{8,16},{9,17... | collective-permute-start | bytes 172040
  473.3 23.8 %collective-permute-start.4 = (f32[8,2048]{1,0:T(8,128)S(1)}, f32[8,2048]{1,0:T(8,128)S(1)}, u32[]{:S(2)}, u32[]{:S(2)}) collective-permute-start(f32[8,2048]{1,0:T(8,128)S(1)} %fusion), channel_id=1, source_target_pairs={{0,5},{1,6},{2,7},{3,8},{4,9},{5,10},{6,11},{7,12},{8,13},{9,14},{... | collective-permute-start | bytes 196616
  479.2 17.9 %collective-permute-start.3 = (f32[8,2048]{1,0:T(8,128)S(1)}, f32[8,2048]{1,0:T(8,128)S(1)}, u32[]{:S(2)}, u32[]{:S(2)}) collective-permute-start(f32[8,2048]{1,0:T(8,128)S(1)} %fusion), channel_id=1, source_target_pairs={{0,4},{1,5},{2,6},{3,7},{4,8},{5,9},{6,10},{7,11},{8,12},{9,13},{1... | collective-permute-start | bytes 196616
  487.8 9.3 %collective-permute-start.2 = (f32[8,2048]{1,0:T(8,128)S(1)}, f32[8,2048]{1,0:T(8,128)S(1)}, u32[]{:S(2)}, u32[]{:S(2)}) collective-permute-start(f32[8,2048]{1,0:T(8,128)S(1)} %fusion), channel_id=1, source_target_pairs={{0,3},{1,4},{2,5},{3,6},{4,7},{5,8},{6,9},{7,10},{8,11},{9,12},{10... | collective-permute-start | bytes 196616
  489.8 9.0 %collective-permute-start.1 = (f32[8,2048]{1,0:T(8,128)S(1)}, f32[8,2048]{1,0:T(8,128)S(1)}, u32[]{:S(2)}, u32[]{:S(2)}) collective-permute-start(f32[8,2048]{1,0:T(8,128)S(1)} %fusion), channel_id=1, source_target_pairs={{0,2},{1,3},{2,4},{3,5},{4,6},{5,7},{6,8},{7,9},{8,10},{9,11},{10,... | collective-permute-start | bytes 196616
  493.2 8.3 %collective-permute-start = (f32[8,2048]{1,0:T(8,128)S(1)}, f32[8,2048]{1,0:T(8,128)S(1)}, u32[]{:S(2)}, u32[]{:S(2)}) collective-permute-start(f32[8,2048]{1,0:T(8,128)S(1)} %fusion), channel_id=1, source_target_pairs={{0,1},{1,2},{2,3},{3,4},{4,5},{5,6},{6,7},{7,8},{8,9},{9,10},{10,1... | collective-permute-start | bytes 196616
Sparse Core Ops, SparseCore 0:
  56.3 120.4 all-gather.6
  179.5 116.2 all-gather.4
where the time goes:
time: 565 us; the launch traced here: 564 us
  blocking collectives  285 us (50%)
  waiting for transfers between devices  191 us (34%)
  starting transfers between devices  44 us (8%)
  between operations  15.6 us (3%)
  matrix products  13 us (2%)
  local copies, waits for them, and re-layouts  12.1 us (2%)
    unnamed x2, blocking collectives  197 us
    all_gather x1, waiting for transfers between devices, local(): grad_rows = lax.all_gather(dy_picked, 'dp', axis=0, tiled=True)  115 us
    all_gather x1, waiting for transfers between devices, local(): input_rows = lax.all_gather(x_picked, 'dp', axis=0, tiled=True)  71.9 us
    all_gather x1, blocking collectives, local(): lax.all_gather(tokens, 'expert', axis=1, tiled=True)  44.1 us
    all_gather x1, blocking collectives, local(): lax.all_gather(out_grad, 'expert', axis=1, tiled=True)  44 us
    unnamed x8, starting transfers between devices  43.9 us
  transfers between devices with their start and end apart: 10, of which 4 were waited for; matrix products, arithmetic and copies ran while one was open for 2% of the time, Pallas kernels for 0%

commit v1 on v0

--- a/solution.py
+++ b/solution.py
@@ -40,7 +40,9 @@
     gate_slab = w_gate[0]
     up_slab = w_up[0]
     down_slab = w_down[0]
-    input_rows = lax.all_gather(x_picked, "dp", axis=0, tiled=True)
+    input_rows = jnp.concatenate(
+        lax.all_to_all(jnp.stack([x_picked] * lax.axis_size("dp")), "dp", 0, 0), axis=0
+    )
     pre_gate = jnp.dot(input_rows, gate_slab, preferred_element_type=jnp.float32)
     pre_up = jnp.dot(input_rows, up_slab, preferred_element_type=jnp.float32)
     sigmoid_gate = jax.nn.sigmoid(pre_gate)

time: 565 us -> 530 us (0.938)
  waiting for transfers between devices: 191 us -> 110 us
  blocking collectives: 285 us -> 316 us
  starting transfers between devices: 44 us -> 57.7 us
    all_gather x1 -> x0, waiting for transfers between devices: 71.9 us -> none  [local(): input_rows = lax.all_gather(x_picked, 'dp', axis=0, tiled=True)]
    all_gather x1, blocking collectives: 44 us -> 75 us  [local(): lax.all_gather(out_grad, 'expert', axis=1, tiled=True)]
    all_to_all x0 -> x1, starting transfers between devices: none -> 13.8 us  [local(): lax.all_to_all(jnp.stack([x_picked] * lax.axis_size('dp')), 'dp', 0, 0)]
    all_gather x1, waiting for transfers between devices: 115 us -> 105 us  [local(): grad_rows = lax.all_gather(dy_picked, 'dp', axis=0, tiled=True)]
  transfers between devices with their start and end apart: 10 -> 10, of which waited for: 4 -> 3; matrix products, arithmetic and copies ran while one was open for 2% -> 2% of each run, Pallas kernels for 0% -> 0%
where the time goes in v1:
time: 530 us; the launch traced here: 529 us
  blocking collectives  316 us (60%)
  waiting for transfers between devices  110 us (21%)
  starting transfers between devices  57.7 us (11%)
  between operations  15.6 us (3%)
  local copies, waits for them, and re-layouts  13.7 us (3%)
  matrix products  12.4 us (2%)
    unnamed x2, blocking collectives  197 us
    all_gather x1, waiting for transfers between devices, local(): grad_rows = lax.all_gather(dy_picked, 'dp', axis=0, tiled=True)  105 us
    all_gather x1, blocking collectives, local(): lax.all_gather(out_grad, 'expert', axis=1, tiled=True)  75 us
    all_gather x1, blocking collectives, local(): lax.all_gather(tokens, 'expert', axis=1, tiled=True)  44.1 us
    unnamed x8, starting transfers between devices  43.9 us
    all_to_all x1, starting transfers between devices, local(): lax.all_to_all(jnp.stack([x_picked] * lax.axis_size('dp')), 'dp', 0, 0)  13.8 us
  transfers between devices with their start and end apart: 10, of which 3 were waited for; matrix products, arithmetic and copies ran while one was open for 2% of the time, Pallas kernels for 0%

profile of v1, /device:TPU:64, one launch (start us, length us, event | category | flops | bytes accessed | tf_op | source)
XLA Modules:
  0.0 528.7 jit_solution(9808620005610312488)
XLA Ops:
  7.2 0.0 copy-start
  7.2 0.7 fusion.29
  7.9 0.7 compare_bitcast_fusion
  8.6 0.7 bitcast_convert_fusion
  9.3 0.7 convert_reduce_fusion
  10.0 0.1 copy.70
  10.0 0.1 copy.72
  10.1 0.1 reshape.53
  10.3 0.0 copy-start.6
  10.3 0.7 gather_fusion
  11.0 0.1 gather.7
  11.1 0.1 copy.73
  11.1 0.0 copy-done.5
  11.2 44.1 %all_gather.11 = bf16[1,16,2048]{2,0,1:T(2,128)(2,1)S(1)} all-gather(bf16[1,2,2048]{2,0,1:T(2,128)(2,1)S(1)} %copy.75), channel_id=1, replica_groups=mesh['expert'=8,'dp'=64] {'expert'}, dimensions={1}, use_global_device_ids=true | all-gather | bytes 73728 | tf_op jit(solution)/shard_map/all_gather | solution.py:23
  55.4 0.2 convolution_convert_fusion.3
  55.5 1.6 stack.2
  57.1 13.8 %all-to-all-start = ((bf16[64,7,2048]{2,1,0:T(8,128)(2,1)}), bf16[64,7,2048]{2,1,0:T(8,128)(2,1)}, u32[]{:S(2)}, u32[]{:S(2)}) async-start(bf16[64,7,2048]{2,1,0:T(8,128)(2,1)} %stack.2), calls=%async_computation | async-start | bytes 4194304 | tf_op jit(solution)/shard_map/all_to_all | solution.py:44
  70.9 0.0 all-gather.3.cloned.1.call-start
  70.9 0.0 copy-done.7
  71.0 75.0 %all_gather.9 = bf16[1,16,2048]{2,0,1:T(2,128)(2,1)S(1)} all-gather(bf16[1,2,2048]{2,0,1:T(2,128)(2,1)S(1)} %copy.74), channel_id=1, replica_groups=mesh['expert'=8,'dp'=64] {'expert'}, dimensions={1}, use_global_device_ids=true | all-gather | bytes 73728 | tf_op jit(solution)/shard_map/all_gather | solution.py:24
  146.0 0.8 fusion.4
  146.7 0.0 all-gather.3.cloned.1.call-update
  146.8 1.3 dynamic-slice.6
  148.0 1.3 dynamic-slice.2
  150.6 0.0 all-to-all-done
  150.6 2.6 reshape.51
  153.2 0.0 copy-done
  153.2 0.0 copy-start.2
  153.2 0.6 fusion.7
  153.9 0.4 copy-done.2
  154.3 0.6 fusion.10
  154.9 105.5 %all-gather.3.cloned.1.call-done = bf16[64,7,2048]{2,1,0:T(8,128)(2,1)} async-done(((bf16[1,7,2048]{2,1,0:T(8,128)(2,1)}), bf16[64,7,2048]{2,1,0:T(8,128)(2,1)}) %all-gather.3.cloned.1.call-update) | async-done | bytes 1835024 | tf_op jit(solution)/shard_map/all_gather | solution.py:51
  260.4 3.7 reshape.61
  264.1 3.0 fusion.3
  267.1 0.0 copy-done.1
  267.1 0.6 multiply_convert_fusion.1
  267.7 0.0 copy-start.3
  267.8 0.6 fusion.5
  268.4 2.4 convolution_add_fusion
  270.9 143.6 %fusion = f32[8,2048]{1,0:T(8,128)S(1)} fusion(f32[448,2048]{1,0:T(8,128)} %convolution_add_fusion), kind=kCustom, calls=%all-reduce-scatter | all-reduce-scatter fusion | flops 1048577 | bytes 3737600
  414.4 0.0 copy-start.4
  414.4 2.1 collective-permute-start.6
  416.5 1.9 collective-permute-start.5
  418.4 17.8 %collective-permute-start.7 = (f32[7,2048]{1,0:T(8,128)S(1)}, f32[7,2048]{1,0:T(8,128)S(1)}, u32[]{:S(2)}, u32[]{:S(2)}) collective-permute-start(f32[7,2048]{1,0:T(8,128)S(1)} %slice.2), channel_id=1, source_target_pairs={{0,8},{1,9},{2,10},{3,11},{4,12},{5,13},{6,14},{7,15},{8,16},{9,17... | collective-permute-start | bytes 172040
  436.3 1.6 fusion.2
  437.9 5.9 %collective-permute-start.4 = (f32[8,2048]{1,0:T(8,128)S(1)}, f32[8,2048]{1,0:T(8,128)S(1)}, u32[]{:S(2)}, u32[]{:S(2)}) collective-permute-start(f32[8,2048]{1,0:T(8,128)S(1)} %fusion), channel_id=1, source_target_pairs={{0,5},{1,6},{2,7},{3,8},{4,9},{5,10},{6,11},{7,12},{8,13},{9,14},{... | collective-permute-start | bytes 196616
  443.8 8.7 %collective-permute-start.3 = (f32[8,2048]{1,0:T(8,128)S(1)}, f32[8,2048]{1,0:T(8,128)S(1)}, u32[]{:S(2)}, u32[]{:S(2)}) collective-permute-start(f32[8,2048]{1,0:T(8,128)S(1)} %fusion), channel_id=1, source_target_pairs={{0,4},{1,5},{2,6},{3,7},{4,8},{5,9},{6,10},{7,11},{8,12},{9,13},{1... | collective-permute-start | bytes 196616
  452.4 0.0 collective-permute-done.7
  452.4 1.9 collective-permute-start.2
  454.4 0.0 collective-permute-done.6
  454.4 3.4 collective-permute-start.1
  457.8 0.0 collective-permute-done.5
  457.8 2.3 collective-permute-start
  460.1 0.0 copy-done.4
  460.1 1.6 fusion.1
  461.7 0.0 collective-permute-done.4
  461.7 0.0 collective-permute-done.3
  461.7 0.0 collective-permute-done.2
  461.7 1.7 collective-permute-done.1
  463.4 2.7 collective-permute-done
  466.0 1.0 concatenate.3
  467.1 0.4 fusion.15
  467.5 53.8 %all-reduce.4 = bf16[16,2048]{1,0:T(8,128)(2,1)S(1)} all-reduce(f32[16,2048]{1,0:T(8,128)S(1)} %fusion.15), channel_id=3, replica_groups=mesh['expert'=8,'dp'=64] {'expert'}, use_global_device_ids=true, to_apply=%region_5.6.clone | all-reduce | flops 32768 | bytes 196608
  521.2 0.6 fusion.22
  (14 shorter events, 0.1 us)
Async XLA Ops:
  7.2 146.0 %copy-start = (bf16[1,2048,128]{2,1,0:T(8,128)(2,1)S(1)}, bf16[1,2048,128]{2,1,0:T(8,128)(2,1)}, u32[]{:S(2)}) copy-start(bf16[1,2048,128]{2,1,0:T(8,128)(2,1)} %param.11) | copy-start | bytes 1572868
  10.2 0.9 copy-start.5
  10.3 0.9 copy-start.6
  57.1 13.8 %copy-start.7 = (bf16[1,2,2048]{2,1,0:T(2,128)(2,1)S(1)}, bf16[1,2,2048]{2,1,0:T(2,128)(2,1)}, u32[]{:S(2)}) copy-start(bf16[1,2,2048]{2,1,0:T(2,128)(2,1)} %param.8) | copy-start | bytes 24580
  57.1 93.5 %all-to-all-start = ((bf16[64,7,2048]{2,1,0:T(8,128)(2,1)}), bf16[64,7,2048]{2,1,0:T(8,128)(2,1)}, u32[]{:S(2)}, u32[]{:S(2)}) async-start(bf16[64,7,2048]{2,1,0:T(8,128)(2,1)} %stack.2), calls=%async_computation | async-start | bytes 4194304 | tf_op jit(solution)/shard_map/all_to_all | solution.py:44
  70.9 189.5 %all-gather.3.cloned.1.call-start = ((), (), s32[]{:S(2)}) async-start(), calls=%async_computation.1 | async-start | bytes 2129920 | tf_op jit(solution)/shard_map/all_gather | solution.py:51
  153.2 1.0 copy-start.2
  264.1 3.0 copy-start.1
  264.1 3.0 copy-start.8
  267.7 0.7 copy-start.3
  414.4 45.7 %copy-start.4 = (bf16[448,128]{1,0:T(8,128)(2,1)S(1)}, bf16[448,128]{1,0:T(8,128)(2,1)}, u32[]{:S(2)}) copy-start(bf16[448,128]{1,0:T(8,128)(2,1)} %copy-done.3) | copy-start | bytes 344068
  414.4 39.9 %collective-permute-start.6 = (f32[8,2048]{1,0:T(8,128)S(1)}, f32[8,2048]{1,0:T(8,128)S(1)}, u32[]{:S(2)}, u32[]{:S(2)}) collective-permute-start(f32[8,2048]{1,0:T(8,128)S(1)} %fusion), channel_id=1, source_target_pairs={{0,7},{1,8},{2,9},{3,10},{4,11},{5,12},{6,13},{7,14},{8,15},{9,16}... | collective-permute-start | bytes 196616
  416.5 41.3 %collective-permute-start.5 = (f32[8,2048]{1,0:T(8,128)S(1)}, f32[8,2048]{1,0:T(8,128)S(1)}, u32[]{:S(2)}, u32[]{:S(2)}) collective-permute-start(f32[8,2048]{1,0:T(8,128)S(1)} %fusion), channel_id=1, source_target_pairs={{0,6},{1,7},{2,8},{3,9},{4,10},{5,11},{6,12},{7,13},{8,14},{9,15},... | collective-permute-start | bytes 196616
  418.4 34.0 %collective-permute-start.7 = (f32[7,2048]{1,0:T(8,128)S(1)}, f32[7,2048]{1,0:T(8,128)S(1)}, u32[]{:S(2)}, u32[]{:S(2)}) collective-permute-start(f32[7,2048]{1,0:T(8,128)S(1)} %slice.2), channel_id=1, source_target_pairs={{0,8},{1,9},{2,10},{3,11},{4,12},{5,13},{6,14},{7,15},{8,16},{9,17... | collective-permute-start | bytes 172040
  437.9 23.8 %collective-permute-start.4 = (f32[8,2048]{1,0:T(8,128)S(1)}, f32[8,2048]{1,0:T(8,128)S(1)}, u32[]{:S(2)}, u32[]{:S(2)}) collective-permute-start(f32[8,2048]{1,0:T(8,128)S(1)} %fusion), channel_id=1, source_target_pairs={{0,5},{1,6},{2,7},{3,8},{4,9},{5,10},{6,11},{7,12},{8,13},{9,14},{... | collective-permute-start | bytes 196616
  443.8 17.9 %collective-permute-start.3 = (f32[8,2048]{1,0:T(8,128)S(1)}, f32[8,2048]{1,0:T(8,128)S(1)}, u32[]{:S(2)}, u32[]{:S(2)}) collective-permute-start(f32[8,2048]{1,0:T(8,128)S(1)} %fusion), channel_id=1, source_target_pairs={{0,4},{1,5},{2,6},{3,7},{4,8},{5,9},{6,10},{7,11},{8,12},{9,13},{1... | collective-permute-start | bytes 196616
  452.4 9.3 %collective-permute-start.2 = (f32[8,2048]{1,0:T(8,128)S(1)}, f32[8,2048]{1,0:T(8,128)S(1)}, u32[]{:S(2)}, u32[]{:S(2)}) collective-permute-start(f32[8,2048]{1,0:T(8,128)S(1)} %fusion), channel_id=1, source_target_pairs={{0,3},{1,4},{2,5},{3,6},{4,7},{5,8},{6,9},{7,10},{8,11},{9,12},{10... | collective-permute-start | bytes 196616
  454.4 9.0 %collective-permute-start.1 = (f32[8,2048]{1,0:T(8,128)S(1)}, f32[8,2048]{1,0:T(8,128)S(1)}, u32[]{:S(2)}, u32[]{:S(2)}) collective-permute-start(f32[8,2048]{1,0:T(8,128)S(1)} %fusion), channel_id=1, source_target_pairs={{0,2},{1,3},{2,4},{3,5},{4,6},{5,7},{6,8},{7,9},{8,10},{9,11},{10,... | collective-permute-start | bytes 196616
  457.8 8.3 %collective-permute-start = (f32[8,2048]{1,0:T(8,128)S(1)}, f32[8,2048]{1,0:T(8,128)S(1)}, u32[]{:S(2)}, u32[]{:S(2)}) collective-permute-start(f32[8,2048]{1,0:T(8,128)S(1)} %fusion), channel_id=1, source_target_pairs={{0,1},{1,2},{2,3},{3,4},{4,5},{5,6},{6,7},{7,8},{8,9},{9,10},{10,1... | collective-permute-start | bytes 196616
Sparse Core Ops, SparseCore 0:
  146.9 113.4 all-gather.2
